TPU v7x, 256 devices: a whole 4x4x8 slice. The times are simulated.
256 devices in a mesh: dp: 8 (over z_hi, x), expert: 32 (over y, z_lo, core).
Axes of the slice: x: 4, y: 4, z: 8 (z_hi: 2, z_lo: 4; z = z_hi * 4 + z_lo), core: 2. Of those that a mesh axis runs over, the one named last changes fastest.
Arguments:
- tokens: bfloat16 [32768, 2048], P(('dp', 'expert')), may hold values from -6 to 6
- gate_weights: float32 [32768, 2], P(('dp', 'expert')), may hold values from 0.02 to 0.5
- expert_ids: int32 [32768, 2], P(('dp', 'expert')), may hold values from 0 to 31, as said below
- hot_experts: int32 [4], replicated, may hold values from 0 to 31, as said below
- gate_proj: bfloat16 [32, 2048, 768], P('expert', 'dp'), may hold values from -0.125 to 0.125
- up_proj: bfloat16 [32, 2048, 768], P('expert', 'dp'), may hold values from -0.125 to 0.125
- down_proj: bfloat16 [32, 2048, 768], P('expert', 'dp'), may hold values from -0.21875 to 0.21875
- out_grad: bfloat16 [32768, 2048], P(('dp', 'expert')), may hold values from -6 to 6
Outputs:
- layer_out: bfloat16 [32768, 2048], P(('dp', 'expert'))
- tokens_grad: bfloat16 [32768, 2048], P(('dp', 'expert'))
- routing_grad: float32 [32768, 2], P(('dp', 'expert'))
- gate_proj_grad: bfloat16 [32, 2048, 768], P('expert', 'dp')
- up_proj_grad: bfloat16 [32, 2048, 768], P('expert', 'dp')
- down_proj_grad: bfloat16 [32, 2048, 768], P('expert', 'dp')
Inputs may be any that keep to these rules, and one draw needn't show every extreme that they name: `expert_ids`: each token names 2 different experts. In each block of 128 rows of one device no expert is named more than 14 times, and the expert hot_experts[0] is named exactly 14 times in every block. `hot_experts`: 4 different experts.
All inputs are finite; a program needn't handle non-finite values.
Results may differ from a plain program's by a relative error of at most 0.012.
Values may be sent and summed in bfloat16 or wider, within the bound.
A program may use at most 128 MiB of HBM per device.

v0:
```python
import jax
import jax.numpy as jnp
from jax import lax
from jax.sharding import PartitionSpec as P

TOPK = 2


def contract_last(left_side, right_side):
    return lax.dot_general(
        left_side, right_side, (((1,), (1,)), ((), ())), preferred_element_type=jnp.float32
    )


def contract_first(left_side, right_side):
    return lax.dot_general(
        left_side, right_side, (((0,), (0,)), ((), ())), preferred_element_type=jnp.float32
    )


def body(tokens, gate_weights, expert_ids, hot_experts, gate_proj, up_proj, down_proj, out_grad):
    owners = lax.axis_size("expert")
    model_width = tokens.shape[1]
    token_count = tokens.shape[0]
    assign_count = token_count * TOPK
    cap_rows = 5 * assign_count // (4 * owners)
    slot_count = cap_rows + assign_count // (2 * owners)
    local_gate = gate_proj[0]
    local_up = up_proj[0]
    local_down = down_proj[0]
    hidden_units = local_gate.shape[1]
    flat_ids = expert_ids.reshape(-1)
    expert_range = jnp.arange(owners, dtype=jnp.int32)
    onehot = (flat_ids[:, None] == expert_range[None, :]).astype(jnp.int32)
    before = jnp.cumsum(onehot, axis=0) - onehot
    slot_pos = jnp.sum(before * onehot, axis=1)
    hot_flags = jnp.sum((hot_experts[:, None] == expert_range[None, :]).astype(jnp.int32), axis=0)
    hot_row = jnp.sum(onehot * hot_flags[None, :], axis=1) > 0
    kept_mask = slot_pos < jnp.where(hot_row, slot_count, cap_rows)
    row_slot = flat_ids * slot_count + jnp.minimum(slot_pos, slot_count - 1)
    target = jnp.where(kept_mask, row_slot, -1)
    placing = (jnp.arange(owners * slot_count, dtype=jnp.int32)[:, None] == target[None, :]).astype(
        jnp.bfloat16
    )
    token_place = placing.reshape(owners * slot_count, token_count, TOPK).sum(axis=2)
    send_rows = jnp.dot(token_place, tokens, preferred_element_type=jnp.float32).astype(
        jnp.bfloat16
    )
    send_rows = send_rows.reshape(owners, slot_count, model_width)
    received = lax.all_to_all(send_rows, "expert", split_axis=0, concat_axis=0, tiled=True)
    expert_expert_rows = received.reshape(-1, model_width)
    pieces = (
        lax.all_gather(local_gate, "dp", axis=0, tiled=True),
        lax.all_gather(local_up, "dp", axis=0, tiled=True),
    )
    columns = expert_expert_rows
    gate_act = jnp.dot(columns, pieces[0], preferred_element_type=jnp.float32)
    up_act = jnp.dot(columns, pieces[1], preferred_element_type=jnp.float32)
    expert_hidden = (gate_act * jax.nn.sigmoid(gate_act) * up_act).astype(jnp.bfloat16)
    output = contract_last(
        expert_hidden, lax.all_gather(local_down, "dp", axis=0, tiled=True)
    ).astype(jnp.bfloat16)
    returned = lax.all_to_all(
        output.reshape(received.shape), "expert", split_axis=0, concat_axis=0, tiled=True
    )
    act_shape = (received.shape[0], received.shape[1], hidden_units)
    returned, saved_rows, saved_gate, saved_up = (
        returned,
        received,
        gate_act.reshape(act_shape),
        up_act.reshape(act_shape),
    )
    safe_slot = jnp.where(kept_mask, row_slot, 0)
    keep_scale = kept_mask.astype(jnp.float32)[:, None]
    chosen = (
        jnp.take(returned.reshape(-1, model_width), safe_slot, axis=0).astype(jnp.float32)
        * keep_scale
    )
    weight_flat = gate_weights.reshape(-1, 1)
    layer_out = (
        (chosen * weight_flat)
        .reshape(token_count, TOPK, model_width)
        .sum(axis=1)
        .astype(jnp.bfloat16)
    )
    routing_grad = jnp.sum(
        chosen.reshape(token_count, TOPK, model_width) * out_grad.astype(jnp.float32)[:, None, :],
        axis=2,
    )
    spread = (weight_flat * jnp.repeat(out_grad, TOPK, axis=0).astype(jnp.float32)).astype(
        jnp.bfloat16
    )
    grad_send = jnp.dot(placing, spread, preferred_element_type=jnp.float32).astype(jnp.bfloat16)
    grad_recv = lax.all_to_all(
        grad_send.reshape(owners, slot_count, model_width),
        "expert",
        split_axis=0,
        concat_axis=0,
        tiled=True,
    )
    grad_in = grad_recv.reshape(-1, model_width)
    expert_rows = saved_rows.reshape(-1, model_width)
    gate_act = saved_gate.reshape(-1, hidden_units)
    up_act = saved_up.reshape(-1, hidden_units)
    columns = grad_in
    grad_hidden = jnp.dot(
        columns,
        lax.all_gather(local_down, "dp", axis=0, tiled=True),
        preferred_element_type=jnp.float32,
    )
    sigmoid_act = jax.nn.sigmoid(gate_act)
    silu_act = gate_act * sigmoid_act
    hidden = (silu_act * up_act).astype(jnp.bfloat16)
    grad_up = (grad_hidden * silu_act).astype(jnp.bfloat16)
    grad_gate = (
        grad_hidden * up_act * sigmoid_act * (1.0 + gate_act * (1.0 - sigmoid_act))
    ).astype(jnp.bfloat16)
    pieces = lax.all_gather((local_gate, local_up), "dp", axis=0, tiled=True)
    grad_rows = (contract_last(grad_gate, pieces[0]) + contract_last(grad_up, pieces[1])).astype(
        jnp.bfloat16
    )
    grad_back = lax.all_to_all(
        grad_rows.reshape(owners, slot_count, model_width),
        "expert",
        split_axis=0,
        concat_axis=0,
        tiled=True,
    )
    chosen_grad = (
        jnp.take(grad_back.reshape(-1, model_width), safe_slot, axis=0).astype(jnp.float32)
        * keep_scale
    )
    tokens_grad = (
        chosen_grad.reshape(token_count, TOPK, model_width).sum(axis=1).astype(jnp.bfloat16)
    )
    summed = lax.psum_scatter(
        jnp.concatenate(
            [
                contract_first(expert_rows, grad_gate),
                contract_first(expert_rows, grad_up),
                contract_first(grad_in, hidden),
            ],
            axis=1,
        ).astype(jnp.bfloat16),
        "dp",
        scatter_dimension=0,
        tiled=True,
    ).astype(jnp.float32)
    gate_proj_grad = summed[:, :hidden_units].astype(jnp.bfloat16)[None]
    up_proj_grad = summed[:, hidden_units : 2 * hidden_units].astype(jnp.bfloat16)[None]
    down_proj_grad = summed[:, 2 * hidden_units :].astype(jnp.bfloat16)[None]
    return (layer_out, tokens_grad, routing_grad, gate_proj_grad, up_proj_grad, down_proj_grad)


def solution(mesh):
    in_specs = (
        P(("dp", "expert"), None),
        P(("dp", "expert"), None),
        P(("dp", "expert"), None),
        P(),
        P("expert", "dp", None),
        P("expert", "dp", None),
        P("expert", "dp", None),
        P(("dp", "expert"), None),
    )
    out_specs = (
        P(("dp", "expert"), None),
        P(("dp", "expert"), None),
        P(("dp", "expert"), None),
        P("expert", "dp", None),
        P("expert", "dp", None),
        P("expert", "dp", None),
    )
    return jax.shard_map(body, mesh=mesh, in_specs=in_specs, out_specs=out_specs, check_vma=False)
```

profile of v0, /device:TPU:1, one launch (start us, length us, event | category | flops | bytes accessed | tf_op | source)
XLA Modules:
  0.0 598.6 jit_solution(308735472371178573)
XLA Ops:
  7.2 0.7 all-gather.11.cloned.1.call-update
  8.0 0.7 all-gather.9.cloned.1.call-update
  8.7 0.8 copy.39
  9.5 0.1 eq.59
  9.6 0.1 eq.63
  9.7 3.4 broadcast_in_dim.51
  13.2 2.7 convert_element_type.84
  15.9 0.6 reduce-window.6
  16.5 0.2 slice_reduce_fusion
  16.8 0.1 copy.44
  16.9 0.1 mul.91
  17.0 0.1 convert_reduce_fusion
  17.1 0.1 select_reduce_fusion
  17.2 2.0 convolution_convert_fusion.3
  19.2 3.6 reshape.124
  22.8 10.3 %all-to-all-start.2 = ((bf16[32,14,2048]{2,1,0:T(8,128)(2,1)}), bf16[32,14,2048]{2,1,0:T(8,128)(2,1)S(1)}, u32[]{:S(2)}, u32[]{:S(2)}) async-start(bf16[32,14,2048]{2,1,0:T(8,128)(2,1)} %reshape.124), calls=%async_computation.2 | async-start | bytes 4194304 | tf_op jit(solution)/shard_map/all_to_all | solution.py:94
  33.2 0.7 all-gather.7.cloned.1.call-update
  33.9 0.2 lt.22
  34.0 0.1 copy.43
  34.1 0.2 min.16
  34.3 0.1 copy.42
  34.4 0.1 fusion.21
  34.4 1.9 convolution_convert_fusion.4
  36.3 3.6 reshape.119
  39.9 80.4 %all-to-all-done.2 = bf16[32,14,2048]{2,1,0:T(8,128)(2,1)S(1)} async-done(((bf16[32,14,2048]{2,1,0:T(8,128)(2,1)}), bf16[32,14,2048]{2,1,0:T(8,128)(2,1)S(1)}, u32[]{:S(2)}, u32[]{:S(2)}) %all-to-all-start.2) | async-done | bytes 1835040 | tf_op jit(solution)/shard_map/all_to_all | solution.py:94
  120.3 5.9 all-to-all-start
  126.2 0.2 reduce-scatter.2.cloned.1.call-start
  126.5 1.5 reshape.125
  128.0 90.3 %all-to-all-done = bf16[32,14,2048]{2,1,0:T(8,128)(2,1)} async-done(((bf16[32,14,2048]{2,1,0:T(8,128)(2,1)}), bf16[32,14,2048]{2,1,0:T(8,128)(2,1)}, u32[]{:S(2)}, u32[]{:S(2)}) %all-to-all-start) | async-done | bytes 1835040 | tf_op jit(solution)/shard_map/all_to_all | solution.py:50
  218.3 3.7 reshape.120
  222.0 4.6 fusion
  226.6 5.1 fusion.6
  231.6 77.4 %all-gather.7.cloned.1.call-done = bf16[1,2048,768]{2,1,0:T(8,128)(2,1)} async-done(((bf16[1,256,768]{2,1,0:T(8,128)(2,1)}), bf16[1,2048,768]{2,1,0:T(8,128)(2,1)}) %all-gather.7.cloned.1.call-update) | async-done | bytes 3145744 | tf_op jit(solution)/shard_map/all_gather | solution.py:53
  309.1 5.3 multiply_convert_fusion.2
  314.4 1.9 convolution_convert_fusion
  316.3 0.1 copy-done.6
  316.4 1.9 convolution_convert_fusion.1
  318.3 1.9 convolution_convert_fusion.2
  320.2 4.5 pad_maximum_fusion
  324.7 3.7 fusion.12
  328.4 1.8 reshape.121
  330.2 5.6 all-to-all-start.1
  335.9 3.7 fusion.4
  339.5 2.9 add_convert_fusion
  342.4 3.6 reshape.126
  346.0 112.7 %all-to-all-done.1 = bf16[32,14,2048]{2,1,0:T(8,128)(2,1)S(1)} async-done(((bf16[32,14,2048]{2,1,0:T(8,128)(2,1)}), bf16[32,14,2048]{2,1,0:T(8,128)(2,1)S(1)}, u32[]{:S(2)}, u32[]{:S(2)}) %all-to-all-start.1) | async-done | bytes 1835040 | tf_op jit(solution)/shard_map/all_to_all | solution.py:63
  458.7 1.3 copy-done.3
  460.0 28.5 %all-to-all-start.3 = ((bf16[32,14,2048]{2,1,0:T(8,128)(2,1)}), bf16[32,14,2048]{2,1,0:T(8,128)(2,1)}, u32[]{:S(2)}, u32[]{:S(2)}) async-start(bf16[32,14,2048]{2,1,0:T(8,128)(2,1)} %reshape.126), calls=%async_computation.3 | async-start | bytes 4194304 | tf_op jit(solution)/shard_map/all_to_all | solution.py:122
  488.5 2.6 reshape.122
  491.1 2.4 gather_fusion
  493.4 70.1 %all-to-all-done.3 = bf16[32,14,2048]{2,1,0:T(8,128)(2,1)} async-done(((bf16[32,14,2048]{2,1,0:T(8,128)(2,1)}), bf16[32,14,2048]{2,1,0:T(8,128)(2,1)}, u32[]{:S(2)}, u32[]{:S(2)}) %all-to-all-start.3) | async-done | bytes 1835040 | tf_op jit(solution)/shard_map/all_to_all | solution.py:122
  563.5 2.5 reshape.127
  566.1 2.4 gather_fusion.1
  568.5 4.1 multiply_reduce_fusion
  572.6 3.5 reshape.123
  576.1 2.2 reshape.128
  578.3 5.1 reduce_sum.72
  583.5 3.8 reduce_sum.73
  587.2 0.1 reduce_sum.75
  587.4 0.6 copy.45
  588.0 1.3 slice_bitcast_fusion
  589.3 0.9 copy.46
  590.3 0.9 copy.47
  591.2 0.9 copy.48
  (40 shorter events, 0.3 us)
Async XLA Ops:
  7.2 27.3 %copy-start = (bf16[128,2048]{1,0:T(8,128)(2,1)S(1)}, bf16[128,2048]{1,0:T(8,128)(2,1)}, u32[]{:S(2)}) copy-start(bf16[128,2048]{1,0:T(8,128)(2,1)} %param.10) | copy-start | bytes 1572868
  7.2 214.8 %all-gather.11.cloned.1.call-start = ((), (), s32[]{:S(2)}) async-start(), calls=%async_computation.8 | async-start | bytes 3538944 | tf_op jit(solution)/shard_map/all_gather | solution.py:61
  7.9 218.6 %all-gather.9.cloned.1.call-start = ((), (), s32[]{:S(2)}) async-start(), calls=%async_computation.7 | async-start | bytes 3538944 | tf_op jit(solution)/shard_map/all_gather | solution.py:54
  13.2 3.6 copy-start.8
  13.2 3.8 copy-start.10
  15.9 3.3 copy-start.2
  22.8 11.5 %copy-start.7 = (s32[128,2]{0,1:T(2,128)S(1)}, s32[128,2]{0,1:T(2,128)}, u32[]{:S(2)}) copy-start(s32[128,2]{0,1:T(2,128)} %param.12) | copy-start | bytes 3076
  22.8 97.5 %all-to-all-start.2 = ((bf16[32,14,2048]{2,1,0:T(8,128)(2,1)}), bf16[32,14,2048]{2,1,0:T(8,128)(2,1)S(1)}, u32[]{:S(2)}, u32[]{:S(2)}) async-start(bf16[32,14,2048]{2,1,0:T(8,128)(2,1)} %reshape.124), calls=%async_computation.2 | async-start | bytes 4194304 | tf_op jit(solution)/shard_map/all_to_all | solution.py:94
  33.1 275.9 %all-gather.7.cloned.1.call-start = ((), (), s32[]{:S(2)}) async-start(), calls=%async_computation.6 | async-start | bytes 3538944 | tf_op jit(solution)/shard_map/all_gather | solution.py:53
  120.3 98.0 %all-to-all-start = ((bf16[32,14,2048]{2,1,0:T(8,128)(2,1)}), bf16[32,14,2048]{2,1,0:T(8,128)(2,1)}, u32[]{:S(2)}, u32[]{:S(2)}) async-start(bf16[32,14,2048]{2,1,0:T(8,128)(2,1)} %reshape.119), calls=%async_computation | async-start | bytes 4194304 | tf_op jit(solution)/shard_map/all_to_all | solution.py:50
  126.2 461.8 %reduce-scatter.2.cloned.1.call-start = ((), (), s32[]{:S(2)}) async-start(), calls=%async_computation.5 | async-start | bytes 10616832 | tf_op jit(solution)/shard_map/reduce_scatter | solution.py:136
  128.0 94.0 %copy-start.5 = (bf16[448,2048]{1,0:T(8,128)(2,1)S(1)}, bf16[448,2048]{1,0:T(8,128)(2,1)}, u32[]{:S(2)}) copy-start(bf16[448,2048]{1,0:T(8,128)(2,1)} %reshape.125) | copy-start | bytes 5505028
  314.4 1.9 copy-start.11
  314.4 3.9 copy-start.12
  314.4 2.0 copy-start.6
  330.2 128.5 %all-to-all-start.1 = ((bf16[32,14,2048]{2,1,0:T(8,128)(2,1)}), bf16[32,14,2048]{2,1,0:T(8,128)(2,1)S(1)}, u32[]{:S(2)}, u32[]{:S(2)}) async-start(bf16[32,14,2048]{2,1,0:T(8,128)(2,1)} %reshape.121), calls=%async_computation.1 | async-start | bytes 4194304 | tf_op jit(solution)/shard_map/all_to_all | solution.py:63
  335.8 3.7 copy-start.9
  335.8 3.7 copy-start.13
  458.7 1.3 copy-start.3
  460.0 103.6 %all-to-all-start.3 = ((bf16[32,14,2048]{2,1,0:T(8,128)(2,1)}), bf16[32,14,2048]{2,1,0:T(8,128)(2,1)}, u32[]{:S(2)}, u32[]{:S(2)}) async-start(bf16[32,14,2048]{2,1,0:T(8,128)(2,1)} %reshape.126), calls=%async_computation.3 | async-start | bytes 4194304 | tf_op jit(solution)/shard_map/all_to_all | solution.py:122
  578.3 5.1 copy-start.4
  587.4 4.7 copy-start.1
Sparse Core Ops, SparseCore 0:
  10.6 109.0 all-gather.10
  122.3 83.0 all-gather.8
  208.0 101.0 all-gather.6
  324.8 224.1 reduce-scatter.1
where the time goes:
time: 600 us; the launch traced here: 599 us
  waiting for transfers between devices  433 us (72%)
  starting transfers between devices  50.7 us (8%)
  local copies, waits for them, and re-layouts  47.8 us (8%)
  matrix products  34.7 us (6%)
  other arithmetic  18.4 us (3%)
  between operations  14.1 us (2%)
    all_to_all x1, waiting for transfers between devices, body(): lax.all_to_all(output.reshape(received.shape), 'expert', split_axis=0, co...  113 us
    all_to_all x1, waiting for transfers between devices, body(): lax.all_to_all(send_rows, 'expert', split_axis=0, concat_axis=0, tiled=True)  90.3 us
    all_to_all x1, waiting for transfers between devices, body(): lax.all_to_all(grad_send.reshape(owners, slot_count, model_width), 'exper...  80.4 us
    all_gather x1, waiting for transfers between devices, body(): lax.all_gather(local_gate, 'dp', axis=0, tiled=True)  77.4 us
    all_to_all x1, waiting for transfers between devices, body(): lax.all_to_all(grad_rows.reshape(owners, slot_count, model_width), 'exper...  70.1 us
    all_to_all x1, starting transfers between devices, body(): lax.all_to_all(grad_rows.reshape(owners, slot_count, model_width), 'exper...  28.5 us
  transfers between devices with their start and end apart: 8, of which 5 were waited for; matrix products, arithmetic and copies ran while one was open for 13% of the time, Pallas kernels for 0%

commit v1 on v0

v1 whole, which is shorter than its diff:
```python
import functools

import jax
import jax.numpy as jnp
from jax import lax
from jax.experimental import pallas as pl
from jax.experimental.pallas import tpu as pltpu
from jax.sharding import PartitionSpec as P

MESH = pl.DeviceIdType.MESH
BF = jnp.bfloat16
F32 = jnp.float32
D = 2048
FF = 768
TOK = 128
NZ = 4
NQ = 8
S = 16
SH = 256
HF = SH // 2
CC = 512


def dot(a, b, ca=1, cb=0):
    return lax.dot_general(a, b, (((ca,), (cb,)), ((), ())), preferred_element_type=F32)


def kernel(
    hot_ref, ids_ref, gw_ref, tok_hbm, og_hbm, wg_hbm, wu_hbm, wd_hbm,
    lo_ref, tg_ref, rg_ref, dg_ref, du_ref, dd_ref,
    tb, ob, mb, px, pg, xr, gr, w, ga, ua, gh, hid, gg, gu, ro, rr, tp, rv, rgb, rgr,
    wgr, r2, r1, rz,
    lsem, zs, zr, ms, mr, ys, yr, vs, vr, gs, grs, ws, wr, qs, qr,
):
    d = lax.axis_index("dp")
    e = lax.axis_index("expert")
    zhi, x = d // 4, d % 4
    y, z, c = e // 8, (e // 2) % 4, e % 2
    q = y * 2 + c
    xp, xm, xo = (x + 1) % 4, (x + 3) % 4, (x + 2) % 4
    zo = 1 - zhi
    dev_xp, dev_xm = (zhi * 4 + xp, e), (zhi * 4 + xm, e)
    dev_zo = (zo * 4 + x, e)

    def dev_z(k):
        return (d, y * 8 + k * 2 + c)

    def dev_q(k):
        return (d, (k // 2) * 8 + z * 2 + k % 2)

    b1 = z - 1 + 2 * (1 - (z + 3) // 4)
    b3 = 3 * (1 - z // 2)
    b2 = 6 - z - b1 - b3
    order = (b1, b2, b3)

    barrier = pltpu.get_barrier_semaphore()
    peers = [dev_xp, dev_xm, dev_zo]
    peers += [dev_z((z + k) % NZ) for k in range(1, NZ)]
    peers += [dev_q((q + k) % NQ) for k in range(1, NQ)]
    for p in peers:
        pl.semaphore_signal(barrier, 1, device_id=p, device_id_type=MESH)
    pl.semaphore_wait(barrier, len(peers))

    def remote(src, dst, ssem, rsem, dev):
        return pltpu.make_async_remote_copy(
            src_ref=src, dst_ref=dst, send_sem=ssem, recv_sem=rsem,
            device_id=dev, device_id_type=MESH,
        )

    weights = (wg_hbm, wu_hbm, wd_hbm)

    def line_copy(a, src, buf, block, slot, target):
        return remote(src, buf.at[block], zs.at[a, slot], zr.at[a, block], dev_z(target))

    def line_start(a, hbm, buf):
        @pl.when(z < NZ - 1)
        def _():
            line_copy(a, hbm, buf, z, 0, z + 1).start()

        @pl.when(z > 0)
        def _():
            line_copy(a, hbm, buf, z, 1, z - 1).start()

    def line_step(a, buf, i):
        b = order[i]
        line_copy(a, buf.at[b], buf, b, 2, z).wait_recv()

        @pl.when((b < z) & (z < NZ - 1))
        def _():
            line_copy(a, buf.at[b], buf, b, 2 + i, z + 1).start()

        @pl.when((b > z) & (z > 0))
        def _():
            line_copy(a, buf.at[b], buf, b, 2 + i, z - 1).start()

    def line_end(a, hbm, buf):
        @pl.when(z < NZ - 1)
        def _():
            line_copy(a, hbm, buf, z, 0, z + 1).wait_send()

        @pl.when(z > 0)
        def _():
            line_copy(a, hbm, buf, z, 1, z - 1).wait_send()

        for i in range(3):
            b = order[i]

            @pl.when(((b < z) & (z < NZ - 1)) | ((b > z) & (z > 0)))
            def _(b=b, i=i):
                line_copy(a, buf.at[b], buf, b, 2 + i, z).wait_send()

    def wcopy(m, kind):
        own = weights[m]
        if kind == 0:
            return remote(own, w.at[m, x, zhi], ws.at[m, 0], wr.at[m, 0], dev_xp)
        if kind == 1:
            return remote(own, w.at[m, x, zhi], ws.at[m, 1], wr.at[m, 1], dev_xm)
        if kind == 2:
            return remote(own, w.at[m, x, zhi], ws.at[m, 2], wr.at[m, 2], dev_zo)
        g, k = (kind - 3) // 4, (kind - 3) % 4
        zh = zhi if g == 0 else zo
        sems = (ws.at[m, kind], wr.at[m, kind])
        if k == 0:
            r = w.at[m, xm, zh, pl.ds(0, HF)]
            return remote(r, r, *sems, dev_xp)
        if k == 1:
            r = w.at[m, xp, zh, pl.ds(HF, HF)]
            return remote(r, r, *sems, dev_xm)
        if k == 2:
            r = w.at[m, x, zh]
            return remote(r, r, *sems, dev_xp)
        r = w.at[m, x, zh]
        return remote(r, r, *sems, dev_xm)

    def wforward(m, g):
        first = (0, 1) if g == 0 else (9, 10)
        wcopy(m, first[0]).wait_recv()
        wcopy(m, 3 + 4 * g).start()
        wcopy(m, first[1]).wait_recv()
        wcopy(m, 4 + 4 * g).start()

    def wpartner(m):
        wcopy(m, 2).wait_recv()
        wcopy(m, 9).start()
        wcopy(m, 10).start()

    def wlast(m):
        for kind in (3, 4, 7, 8):
            wcopy(m, kind).wait_recv()

    line_start(0, tok_hbm, tb)
    for m in range(3):
        wcopy(m, 2).start()
        wcopy(m, 0).start()
        wcopy(m, 1).start()
    local = [
        pltpu.make_async_copy(tok_hbm, tb.at[z], lsem.at[0]),
        pltpu.make_async_copy(og_hbm, ob.at[z], lsem.at[1]),
    ]
    local += [pltpu.make_async_copy(weights[m], w.at[m, x, zhi], lsem.at[2 + m]) for m in range(3)]
    for cp in local:
        cp.start()

    ids0, ids1 = ids_ref[0:1, :], ids_ref[1:2, :]
    erow = lax.broadcasted_iota(jnp.int32, (32, TOK), 0)
    oh0 = (erow == ids0).astype(F32)
    oh1 = (erow == ids1).astype(F32)
    before = (
        lax.broadcasted_iota(jnp.int32, (TOK, TOK), 0)
        < lax.broadcasted_iota(jnp.int32, (TOK, TOK), 1)
    ).astype(F32)
    count = dot((oh0 + oh1).astype(BF), before.astype(BF))
    hot = (erow == hot_ref[0]) | (erow == hot_ref[1]) | (erow == hot_ref[2]) | (erow == hot_ref[3])
    room = jnp.where(hot, 14.0, 10.0)
    for k, oh, ids, here in ((0, oh0, ids0, count), (1, oh1, ids1, count + oh0)):
        slot = jnp.sum(oh * here, axis=0, keepdims=True)
        most = jnp.sum(oh * room, axis=0, keepdims=True)
        mb[z, k : k + 1, :] = jnp.where(slot < most, ids.astype(F32) * S + slot, -1.0)
        mb[z, 2 + k : 3 + k, :] = gw_ref[k : k + 1, :]
    mb[z, 4:8, :] = jnp.zeros((4, TOK), F32)

    def mcopy(k):
        return remote(mb.at[z], mb.at[z], ms.at[k], mr.at[k], dev_z((z + k) % NZ))

    for k in range(1, NZ):
        mcopy(k).start()

    def places(b):
        r = lax.broadcasted_iota(jnp.int32, (TOK, TOK), 0)
        code = ((r // 32) * 8 + z * 2 + (r // 16) % 2) * S + r % 16
        code = code.astype(F32)
        p0 = (code == mb[b, 0:1, :]).astype(F32)
        p1 = (code == mb[b, 1:2, :]).astype(F32)
        return p0, p1

    def ycopy(a, src, dst, b, k):
        return remote(src.at[(q + k) % NQ, b], dst.at[q, b], ys.at[a, k], yr.at[a, k], dev_q((q + k) % NQ))

    def ywhole(a, src, dst, k):
        return remote(src.at[(q + k) % NQ], dst.at[q], ys.at[a, k], yr.at[a, k], dev_q((q + k) % NQ))

    def pack(a, b):
        p0, p1 = places(b)
        pm = (p0 + p1).astype(BF)
        if a == 1:
            weight = jnp.sum(p0 * mb[b, 2:3, :] + p1 * mb[b, 3:4, :], axis=1, keepdims=True)
        src, dst, inp = (px, xr, tb) if a == 0 else (pg, gr, ob)

        @pl.loop(0, D // CC)
        def _(j):
            cols = pl.ds(pl.multiple_of(j * CC, CC), CC)
            rows = dot(pm, inp[b, :, cols])
            if a == 1:
                rows = rows * weight
            src[:, b, :, cols] = rows.astype(BF).reshape(NQ, S, CC)

        for k in range(1, NQ):
            ycopy(a, src, dst, b, k).start()
        dst[q, b] = src[q, b]

    local[0].wait()
    pack(0, z)
    for k in range(1, NZ):
        mcopy(k).wait_recv()
    line_step(0, tb, 0)
    pack(0, order[0])
    wforward(0, 0)
    line_step(0, tb, 1)
    pack(0, order[1])
    line_start(1, og_hbm, ob)
    wforward(1, 0)
    line_step(0, tb, 2)
    pack(0, order[2])
    wforward(2, 0)
    local[1].wait()
    pack(1, z)
    wpartner(0)
    line_step(1, ob, 0)
    pack(1, order[0])
    wpartner(1)
    line_step(1, ob, 1)
    pack(1, order[1])
    wpartner(2)
    wforward(0, 1)
    wforward(1, 1)
    line_step(1, ob, 2)
    pack(1, order[2])
    wforward(2, 1)
    for m in range(3):
        local[2 + m].wait()

    def ywait(a, src, dst):
        for k in range(1, NQ):
            ywhole(a, src, dst, k).wait_recv()

    def shard(j):
        return pl.ds(pl.multiple_of(j * SH, SH), SH)

    def rows_by(buf, j):
        return buf[:, :, :, shard(j)].reshape(NQ * NZ * S, SH)

    def through(acc, buf, m):
        acc[...] = dot(rows_by(buf, 0), w[m, 0, 0])

        @pl.loop(1, 8)
        def _(j):
            acc[...] += dot(rows_by(buf, j), w[m, j % 4, j // 4])

    ywait(0, px, xr)
    wlast(0)
    through(ga, xr, 0)
    wlast(1)
    through(ua, xr, 1)

    RB = 64

    @pl.loop(0, 512 // RB)
    def _(i):
        rs = pl.ds(pl.multiple_of(i * RB, RB), RB)
        g = ga[rs, :]
        hid[rs, :] = (g * jax.nn.sigmoid(g) * ua[rs, :]).astype(BF)

    wlast(2)
    for k in range(1, NQ):
        ywhole(0, px, xr, k).wait_send()

    @pl.loop(0, 8)
    def _(j):
        rows = dot(hid[...], w[2, j % 4, j // 4], 1, 1).astype(BF)
        px[:, :, :, shard(j)] = rows.reshape(NQ, NZ, S, SH)

    def yback(a, src, dst, k):
        t = (q + k) % NQ
        return remote(src.at[t], dst.at[q], ys.at[2 + a, k], yr.at[2 + a, k], dev_q(t))

    for k in range(1, NQ):
        yback(0, px, ro, k).start()
    ro[q] = px[q]

    ywait(1, pg, gr)
    through(gh, gr, 2)

    @pl.loop(0, 512 // RB)
    def _(i):
        rs = pl.ds(pl.multiple_of(i * RB, RB), RB)
        g, t = ga[rs, :], gh[rs, :]
        s = jax.nn.sigmoid(g)
        gu[rs, :] = (t * (g * s)).astype(BF)
        gg[rs, :] = (t * ua[rs, :] * s * (1.0 + g * (1.0 - s))).astype(BF)

    pairs = ((xr, gg), (xr, gu), (gr, hid))

    def grads(m, xx):
        left, right = pairs[m]

        @pl.loop(0, 2)
        def _(zh):
            wgr[m, xx, zh] = dot(rows_by(left, zh * 4 + xx), right[...], 0, 0).astype(BF)

    A, B = pl.ds(0, HF), pl.ds(HF, HF)

    def gcopy(m, kind):
        sems = (qs.at[m, kind], qr.at[m, kind])
        if kind == 0:
            return remote(wgr.at[m, xo, :, A], r2.at[m, 0], *sems, dev_xp)
        if kind == 1:
            return remote(wgr.at[m, xo, :, B], r2.at[m, 1], *sems, dev_xm)
        if kind == 2:
            return remote(wgr.at[m, xp, :, B], r1.at[m, 0, :, B], *sems, dev_xp)
        if kind == 3:
            return remote(wgr.at[m, xm, :, A], r1.at[m, 1, :, A], *sems, dev_xm)
        if kind == 4:
            return remote(wgr.at[m, xp, :, A], r1.at[m, 0, :, A], *sems, dev_xp)
        if kind == 5:
            return remote(wgr.at[m, xm, :, B], r1.at[m, 1, :, B], *sems, dev_xm)
        return remote(wgr.at[m, x, zo], rz.at[m], *sems, dev_zo)

    turn = (2, 0, 1)
    for m in turn:
        grads(m, xo)
        gcopy(m, 0).start()
        gcopy(m, 1).start()
    for m in turn:
        grads(m, xp)
        gcopy(m, 2).start()
        grads(m, xm)
        gcopy(m, 3).start()

    for k in range(1, NQ):
        ywhole(1, pg, gr, k).wait_send()

    @pl.loop(0, 8)
    def _(j):
        rows = dot(gg[...], w[0, j % 4, j // 4], 1, 1) + dot(gu[...], w[1, j % 4, j // 4], 1, 1)
        pg[:, :, :, shard(j)] = rows.astype(BF).reshape(NQ, NZ, S, SH)

    for k in range(1, NQ):
        yback(1, pg, rr, k).start()
    rr[q] = pg[q]
    for m in turn:
        grads(m, x)

    def merge(m):
        gcopy(m, 0).wait_recv()
        for zh in range(2):
            wgr[m, xp, zh, A] = (wgr[m, xp, zh, A].astype(F32) + r2[m, 0, zh].astype(F32)).astype(BF)
        gcopy(m, 4).start()
        gcopy(m, 1).wait_recv()
        for zh in range(2):
            wgr[m, xm, zh, B] = (wgr[m, xm, zh, B].astype(F32) + r2[m, 1, zh].astype(F32)).astype(BF)
        gcopy(m, 5).start()

    def collect(m):
        for kind in (2, 3, 4, 5):
            gcopy(m, kind).wait_recv()
        for zh in (zo, zhi):
            for half in (A, B):
                wgr[m, x, zh, half] = (
                    wgr[m, x, zh, half].astype(F32)
                    + r1[m, 0, zh, half].astype(F32)
                    + r1[m, 1, zh, half].astype(F32)
                ).astype(BF)
        gcopy(m, 6).start()

    outs = (dg_ref, du_ref, dd_ref)

    def finish(m):
        gcopy(m, 6).wait_recv()
        outs[m][...] = (wgr[m, x, zhi].astype(F32) + rz[m].astype(F32)).astype(BF)

    line_end(0, tok_hbm, tb)

    def spread(a, b):
        p0, p1 = places(b)
        src, dst = (ro, tb) if a == 0 else (rr, tp)
        if a == 0:
            pw = p0 * mb[b, 2:3, :] + p1 * mb[b, 3:4, :]
            high = pw.astype(BF)
            low = (pw - high.astype(F32)).astype(BF)

            def near(j, acc):
                cols = pl.ds(pl.multiple_of(j * CC, CC), CC)
                return acc + dot(src[:, b, :, cols].reshape(TOK, CC), ob[b, :, cols], 1, 1)

            inner = lax.fori_loop(0, D // CC, near, jnp.zeros((TOK, TOK), F32))
            rgb[b, 0:1, :] = jnp.sum(p0 * inner, axis=0, keepdims=True)
            rgb[b, 1:2, :] = jnp.sum(p1 * inner, axis=0, keepdims=True)
        else:
            high = (p0 + p1).astype(BF)

        @pl.loop(0, D // CC)
        def _(j):
            cols = pl.ds(pl.multiple_of(j * CC, CC), CC)
            rows = src[:, b, :, cols].reshape(TOK, CC)
            total = dot(high, rows, 0, 0)
            if a == 0:
                total = total + dot(low, rows, 0, 0)
            dst[b, :, cols] = total.astype(BF)

    def vright(a, t):
        buf = tb if a == 0 else tp
        return remote(buf.at[t], rv.at[a, t], vs.at[a, t], vr.at[a, t], dev_z(z + 1))

    def vleft(a, t):
        buf = tb if a == 0 else tp
        slot = jnp.where(t < z - 1, t, NZ)
        return remote(buf.at[t], rv.at[a, slot], vs.at[a, t], vr.at[a, slot], dev_z(z - 1))

    def arrived(a, slot):
        buf = tb if a == 0 else tp
        remote(buf.at[0], rv.at[a, slot], vs.at[a, 0], vr.at[a, slot], dev_z(z)).wait_recv()

    def add(a, t, slot):
        buf = tb if a == 0 else tp
        buf[t] = (buf[t].astype(F32) + rv[a, slot].astype(F32)).astype(BF)

    def vstep(a, dist):
        t = z + dist

        @pl.when(t < NZ)
        def _():
            @pl.when(z > 0)
            def _():
                arrived(a, t)
                add(a, t, t)

            vright(a, t).start()

        u = z - dist

        @pl.when(u >= 0)
        def _():
            @pl.when(z < NZ - 1)
            def _():
                arrived(a, u)
                add(a, u, u)

            vleft(a, u).start()

    def vend(a, out):
        buf = tb if a == 0 else tp

        @pl.when(z > 0)
        def _():
            arrived(a, z)
            add(a, z, z)

        @pl.when(z < NZ - 1)
        def _():
            arrived(a, NZ)
            add(a, z, NZ)

        out[...] = buf[z]

    def vsent(a):
        for dist in range(1, NZ):

            @pl.when(z + dist < NZ)
            def _(dist=dist):
                vright(a, z + dist).wait_send()

            @pl.when(z - dist >= 0)
            def _(dist=dist):
                vleft(a, z - dist).wait_send()

    def rgcopy(k):
        t = (z + k) % NZ
        return remote(rgb.at[t], rgr.at[k], gs.at[k], grs.at[k], dev_z(t))

    for b in range(NZ):
        rgb[b] = jnp.zeros((8, TOK), F32)
    for k in range(1, NQ):
        yback(0, px, ro, k).wait_recv()
    for i in (2, 1, 0):
        spread(0, order[i])
    spread(0, z)
    for k in range(1, NZ):
        rgcopy(k).start()
    vstep(0, 3)
    for m in turn:
        merge(m)
    vstep(0, 2)
    vstep(0, 1)
    for k in range(1, NQ):
        yback(1, pg, rr, k).wait_recv()
    for i in (2, 1, 0):
        spread(1, order[i])
    spread(1, z)
    vstep(1, 3)
    collect(turn[0])
    vstep(1, 2)
    vstep(1, 1)
    collect(turn[1])
    vend(0, lo_ref)
    for k in range(1, NZ):
        rgcopy(k).wait_recv()
    rg_ref[...] = (
        rgb[z, 0:2, :] + rgr[1, 0:2, :] + rgr[2, 0:2, :] + rgr[3, 0:2, :]
    )
    vend(1, tg_ref)
    collect(turn[2])
    for m in turn:
        finish(m)

    line_end(1, og_hbm, ob)
    for k in range(1, NZ):
        mcopy(k).wait_send()
        rgcopy(k).wait_send()
    for k in range(1, NQ):
        yback(0, px, ro, k).wait_send()
        yback(1, pg, rr, k).wait_send()
    vsent(0)
    vsent(1)
    for m in range(3):
        for kind in (0, 1, 2, 3, 4, 7, 8, 9, 10):
            wcopy(m, kind).wait_send()
        for kind in range(7):
            gcopy(m, kind).wait_send()


def step(tokens, gate_weights, expert_ids, hot_experts, gate_proj, up_proj, down_proj, out_grad):
    hbm = pl.BlockSpec(memory_space=pl.ANY)
    vmem = pl.BlockSpec(memory_space=pltpu.VMEM)
    smem = pl.BlockSpec(memory_space=pltpu.SMEM)
    rows4 = (NQ, NZ, S, D)
    dma = pltpu.SemaphoreType.DMA
    scratch = [
        pltpu.VMEM((NZ, TOK, D), BF),
        pltpu.VMEM((NZ, TOK, D), BF),
        pltpu.VMEM((NZ, 8, TOK), F32),
        pltpu.VMEM(rows4, BF),
        pltpu.VMEM(rows4, BF),
        pltpu.VMEM(rows4, BF),
        pltpu.VMEM(rows4, BF),
        pltpu.VMEM((3, 4, 2, SH, FF), BF),
        pltpu.VMEM((512, FF), F32),
        pltpu.VMEM((512, FF), F32),
        pltpu.VMEM((512, FF), F32),
        pltpu.VMEM((512, FF), BF),
        pltpu.VMEM((512, FF), BF),
        pltpu.VMEM((512, FF), BF),
        pltpu.VMEM(rows4, BF),
        pltpu.VMEM(rows4, BF),
        pltpu.VMEM((NZ, TOK, D), BF),
        pltpu.VMEM((2, NZ + 1, TOK, D), BF),
        pltpu.VMEM((NZ, 8, TOK), F32),
        pltpu.VMEM((NZ, 8, TOK), F32),
        pltpu.VMEM((3, 4, 2, SH, FF), BF),
        pltpu.VMEM((3, 2, 2, HF, FF), BF),
        pltpu.VMEM((3, 2, 2, SH, FF), BF),
        pltpu.VMEM((3, SH, FF), BF),
        dma((5,)),
        dma((2, 5)),
        dma((2, NZ)),
        dma((NZ,)),
        dma((NZ,)),
        dma((4, NQ)),
        dma((4, NQ)),
        dma((2, NZ)),
        dma((2, NZ + 1)),
        dma((NZ,)),
        dma((NZ,)),
        dma((3, 11)),
        dma((3, 11)),
        dma((3, 7)),
        dma((3, 7)),
    ]
    shard = jax.ShapeDtypeStruct((SH, FF), BF)
    lo, tg, rg, dg, du, dd = pl.pallas_call(
        kernel,
        out_shape=(
            jax.ShapeDtypeStruct((TOK, D), BF),
            jax.ShapeDtypeStruct((TOK, D), BF),
            jax.ShapeDtypeStruct((2, TOK), F32),
            shard,
            shard,
            shard,
        ),
        in_specs=[smem, vmem, vmem, hbm, hbm, hbm, hbm, hbm],
        out_specs=(vmem,) * 6,
        scratch_shapes=scratch,
        compiler_params=pltpu.CompilerParams(
            collective_id=0, has_side_effects=True, vmem_limit_bytes=64 << 20
        ),
    )(
        hot_experts, expert_ids.T, gate_weights.T, tokens, out_grad,
        gate_proj[0], up_proj[0], down_proj[0],
    )
    return lo, tg, rg.T, dg[None], du[None], dd[None]


def solution(mesh):
    rows = P(("dp", "expert"), None)
    mats = P("expert", "dp", None)
    return jax.shard_map(
        step,
        mesh=mesh,
        in_specs=(rows, rows, rows, P(), mats, mats, mats, rows),
        out_specs=(rows, rows, rows, mats, mats, mats),
        check_vma=False,
    )
```

time: 600 us -> 322 us (0.54)
  waiting for transfers between devices: 433 us -> 0 us
  Pallas kernels: 0 us -> 315 us
  starting transfers between devices: 50.7 us -> 0 us
  local copies, waits for them, and re-layouts: 47.8 us -> 6.32 us
  matrix products: 34.7 us -> 0 us
  other arithmetic: 18.4 us -> 0 us
  between operations: 14.1 us -> 0.66 us
    all_to_all x4 -> x0, waiting for transfers between devices: 353 us -> none  [the longest x1 113 us: body(): lax.all_to_all(output.reshape(received.shape), 'expert', split_axis=0, co...]
    pallas_call x0 -> x1, Pallas kernels: none -> 315 us  [step(): pl.pallas_call(kernel, out_shape=(jax.ShapeDtypeStruct((TOK, D), BF), jax...]
    all_gather x3 -> x0, waiting for transfers between devices: 77.4 us -> none  [the longest x1 77.4 us: body(): lax.all_gather(local_gate, 'dp', axis=0, tiled=True)]
    all_to_all x4 -> x0, starting transfers between devices: 50.3 us -> none  [the longest x1 28.5 us: body(): lax.all_to_all(grad_rows.reshape(owners, slot_count, model_width), 'exper...]
    dot_general x11 -> x0, matrix products: 34.7 us -> none  [the longest x3 10.3 us: contract_last(): lax.dot_general(left_side, right_side, (((1,), (1,)), ((), ())), preferre...]
    reshape x10 -> x0, local copies, waits for them, and re-layouts: 28.7 us -> none  [the longest x1 3.67 us: body(): expert_expert_rows = received.reshape(-1, model_width)]
    reduce_sum x6 -> x0, other arithmetic: 13.3 us -> none  [the longest x1 5.11 us: body(): layer_out = (chosen * weight_flat).reshape(token_count, TOPK, model_width...]
  transfers between devices with their start and end apart: 8 -> 0, of which waited for: 5 -> 0; matrix products, arithmetic and copies ran while one was open for 13% -> 0% of each run, Pallas kernels for 0% -> 0%
where the time goes in v1:
time: 322 us
  Pallas kernels  315 us (98%)
  local copies, waits for them, and re-layouts  6.32 us (2%)
    pallas_call x1, Pallas kernels, step(): pl.pallas_call(kernel, out_shape=(jax.ShapeDtypeStruct((TOK, D), BF), jax...  315 us

profile of v1, /device:TPU:1, one launch (start us, length us, event | category | flops | bytes accessed | tf_op | source)
XLA Modules:
  0.0 321.8 jit_solution(14194596985463012977)
XLA Ops:
  0.6 314.8 %shard_map.127 = (bf16[128,2048]{1,0:T(8,128)(2,1)}, bf16[128,2048]{1,0:T(8,128)(2,1)}, f32[2,128]{1,0:T(2,128)}, bf16[256,768]{1,0:T(8,128)(2,1)}, bf16[256,768]{1,0:T(8,128)(2,1)}, /*index=5*/bf16[256,768]{1,0:T(8,128)(2,1)}) custom-call(s32[4]{0:T(128)} %hot_ref.1, s32[2,128]{1,0:T(2,128)} %bitcast.15, f32[2,128]{1,0:T(2,128)} %bitcast.16, ...), custom_call_target="tpu_custom_call" | custom-call | tf_op jit(solution)/shard_map/pallas_call | solution.py:589
  315.4 0.0 copy-start
  315.4 1.9 copy.20
  317.4 0.0 copy-done
  317.4 0.0 copy-start.4
  317.4 0.0 copy-start.3
  317.4 0.8 copy.21
  318.2 0.0 copy-done.4
  318.2 0.6 copy.22
  318.7 0.0 copy-done.3
  318.7 0.0 copy-start.2
  318.7 0.7 copy.23
  319.5 0.4 copy-done.2
  319.9 0.0 copy-start.1
  319.9 0.7 copy.24
  320.6 0.4 copy-done.1
  321.0 0.7 copy.25
Async XLA Ops:
  315.4 2.0 copy-start
  317.4 0.8 copy-start.4
  317.4 1.4 copy-start.3
  318.7 1.1 copy-start.2
  319.9 1.1 copy-start.1

commit v2 on v1

v2 whole, which is shorter than its diff:
```python
import jax
import jax.numpy as jnp
from jax import lax
from jax.experimental import pallas as pl
from jax.experimental.pallas import tpu as pltpu
from jax.sharding import PartitionSpec as P

MESH = pl.DeviceIdType.MESH
BF = jnp.bfloat16
F32 = jnp.float32
D = 2048
FF = 768
TOK = 128
NZ = 4
NQ = 8
S = 16
SH = 256
HF = SH // 2
CC = 512


def dot(a, b, ca=1, cb=0):
    return lax.dot_general(a, b, (((ca,), (cb,)), ((), ())), preferred_element_type=F32)


def kernel(
    hot_ref, ids_ref, gw_ref, tok_hbm, og_hbm, wg_hbm, wu_hbm, wd_hbm,
    lo_ref, tg_ref, rg_ref, dg_ref, du_ref, dd_ref,
    tb, ob, mb, px, pg, xr, gr, w, ga, ua, gh, hid, gg, gu, ro, rr, tp, rv, rgb, rgr,
    wgr, r2, r1, rz,
    lsem, zs, zr, ms, mr, ys, yr, vs, vr, gs, grs, ws, wr, qs, qr,
):
    d = lax.axis_index("dp")
    e = lax.axis_index("expert")
    zhi, x = d // 4, d % 4
    y, z, c = e // 8, (e // 2) % 4, e % 2
    q = y * 2 + c
    xp, xm, xo = (x + 1) % 4, (x + 3) % 4, (x + 2) % 4
    zo = 1 - zhi
    dev_xp, dev_xm = (zhi * 4 + xp, e), (zhi * 4 + xm, e)
    dev_zo = (zo * 4 + x, e)

    ring = zhi * 4 + z
    ahead = 1 - 2 * c

    def dev_z(k):
        p = (ring + ahead * k + 8) % 8
        return ((p // 4) * 4 + x, y * 8 + (p % 4) * 2 + c)

    def dev_q(k):
        return (d, (k // 2) * 8 + z * 2 + k % 2)

    barrier = pltpu.get_barrier_semaphore()
    peers = [dev_xp, dev_xm, dev_zo]
    peers += [dev_z(k) for k in (1, -1, 2, -2)]
    peers += [dev_q((q + k) % NQ) for k in range(1, NQ)]
    for p in peers:
        pl.semaphore_signal(barrier, 1, device_id=p, device_id_type=MESH)
    pl.semaphore_wait(barrier, len(peers))

    def remote(src, dst, ssem, rsem, dev):
        return pltpu.make_async_remote_copy(
            src_ref=src, dst_ref=dst, send_sem=ssem, recv_sem=rsem,
            device_id=dev, device_id_type=MESH,
        )

    weights = (wg_hbm, wu_hbm, wd_hbm)

    def line_copy(a, n):
        src, buf = (tok_hbm, tb) if a == 0 else (og_hbm, ob)
        if n == 3:
            return remote(buf.at[1], buf.at[3], zs.at[a, 3], zr.at[a, 3], dev_z(1))
        return remote(src, buf.at[n], zs.at[a, n], zr.at[a, n], dev_z(1 if n == 1 else -1))

    def line_start(a):
        line_copy(a, 1).start()
        line_copy(a, 2).start()

    def line_step(a, n):
        line_copy(a, n).wait_recv()
        if n == 1:
            line_copy(a, 3).start()

    def line_end(a):
        for n in (1, 2, 3):
            line_copy(a, n).wait_send()

    def wcopy(m, kind):
        own = weights[m]
        if kind == 0:
            return remote(own, w.at[m, x, zhi], ws.at[m, 0], wr.at[m, 0], dev_xp)
        if kind == 1:
            return remote(own, w.at[m, x, zhi], ws.at[m, 1], wr.at[m, 1], dev_xm)
        if kind == 2:
            return remote(own, w.at[m, x, zhi], ws.at[m, 2], wr.at[m, 2], dev_zo)
        g, k = (kind - 3) // 4, (kind - 3) % 4
        zh = zhi if g == 0 else zo
        sems = (ws.at[m, kind], wr.at[m, kind])
        if k == 0:
            r = w.at[m, xm, zh, pl.ds(0, HF)]
            return remote(r, r, *sems, dev_xp)
        if k == 1:
            r = w.at[m, xp, zh, pl.ds(HF, HF)]
            return remote(r, r, *sems, dev_xm)
        if k == 2:
            r = w.at[m, x, zh]
            return remote(r, r, *sems, dev_xp)
        r = w.at[m, x, zh]
        return remote(r, r, *sems, dev_xm)

    def wforward(m, g):
        first = (0, 1) if g == 0 else (9, 10)
        wcopy(m, first[0]).wait_recv()
        wcopy(m, 3 + 4 * g).start()
        wcopy(m, first[1]).wait_recv()
        wcopy(m, 4 + 4 * g).start()

    def wpartner(m):
        wcopy(m, 2).wait_recv()
        wcopy(m, 9).start()
        wcopy(m, 10).start()

    def wlast(m):
        for kind in (3, 4, 7, 8):
            wcopy(m, kind).wait_recv()

    line_start(0)
    for m in range(3):
        if m == 0:
            wcopy(m, 2).start()
        wcopy(m, 0).start()
        wcopy(m, 1).start()
    local = [
        pltpu.make_async_copy(tok_hbm, tb.at[0], lsem.at[0]),
        pltpu.make_async_copy(og_hbm, ob.at[0], lsem.at[1]),
    ]
    local += [pltpu.make_async_copy(weights[m], w.at[m, x, zhi], lsem.at[2 + m]) for m in range(3)]
    for cp in local:
        cp.start()

    ids0, ids1 = ids_ref[0:1, :], ids_ref[1:2, :]
    erow = lax.broadcasted_iota(jnp.int32, (32, TOK), 0)
    oh0 = (erow == ids0).astype(F32)
    oh1 = (erow == ids1).astype(F32)
    before = (
        lax.broadcasted_iota(jnp.int32, (TOK, TOK), 0)
        < lax.broadcasted_iota(jnp.int32, (TOK, TOK), 1)
    ).astype(F32)
    count = dot((oh0 + oh1).astype(BF), before.astype(BF))
    hot = (erow == hot_ref[0]) | (erow == hot_ref[1]) | (erow == hot_ref[2]) | (erow == hot_ref[3])
    room = jnp.where(hot, 14.0, 10.0)
    for k, oh, ids, here in ((0, oh0, ids0, count), (1, oh1, ids1, count + oh0)):
        slot = jnp.sum(oh * here, axis=0, keepdims=True)
        most = jnp.sum(oh * room, axis=0, keepdims=True)
        mb[0, k : k + 1, :] = jnp.where(slot < most, ids.astype(F32) * S + slot, -1.0)
        mb[0, 2 + k : 3 + k, :] = gw_ref[k : k + 1, :]
    mb[0, 4:8, :] = jnp.zeros((4, TOK), F32)

    def mcopy(k):
        return remote(mb.at[0], mb.at[k], ms.at[k], mr.at[k], dev_z((1, -1, 2)[k - 1]))

    for k in range(1, NZ):
        mcopy(k).start()

    def places(b):
        r = lax.broadcasted_iota(jnp.int32, (TOK, TOK), 0)
        code = ((r // 32) * 8 + z * 2 + (r // 16) % 2) * S + r % 16
        code = code.astype(F32)
        p0 = (code == mb[b, 0:1, :]).astype(F32)
        p1 = (code == mb[b, 1:2, :]).astype(F32)
        return p0, p1

    def ycopy(a, src, dst, b, k):
        return remote(src.at[(q + k) % NQ, b], dst.at[q, b], ys.at[a, k], yr.at[a, k], dev_q((q + k) % NQ))

    def ywhole(a, src, dst, k):
        return remote(src.at[(q + k) % NQ], dst.at[q], ys.at[a, k], yr.at[a, k], dev_q((q + k) % NQ))

    def pack(a, b):
        p0, p1 = places(b)
        pm = (p0 + p1).astype(BF)
        if a == 1:
            weight = jnp.sum(p0 * mb[b, 2:3, :] + p1 * mb[b, 3:4, :], axis=1, keepdims=True)
        src, dst, inp = (px, xr, tb) if a == 0 else (pg, gr, ob)

        @pl.loop(0, D // CC)
        def _(j):
            cols = pl.ds(pl.multiple_of(j * CC, CC), CC)
            rows = dot(pm, inp[b, :, cols])
            if a == 1:
                rows = rows * weight
            src[:, b, :, cols] = rows.astype(BF).reshape(NQ, S, CC)

        for k in range(1, NQ):
            ycopy(a, src, dst, b, k).start()
        dst[q, b] = src[q, b]

    def ywait(a, src, dst):
        for k in range(1, NQ):
            ywhole(a, src, dst, k).wait_recv()

    def shard(j):
        return pl.ds(pl.multiple_of(j * SH, SH), SH)

    def rows_by(buf, j):
        return buf[:, :, :, shard(j)].reshape(NQ * NZ * S, SH)

    def through(acc, buf, m):
        acc[...] = dot(rows_by(buf, 0), w[m, 0, 0])

        @pl.loop(1, 8)
        def _(j):
            acc[...] += dot(rows_by(buf, j), w[m, j % 4, j // 4])

    RB = 64

    def hidden_rows():
        @pl.loop(0, 512 // RB)
        def _(i):
            rs = pl.ds(pl.multiple_of(i * RB, RB), RB)
            g = ga[rs, :]
            hid[rs, :] = (g * jax.nn.sigmoid(g) * ua[rs, :]).astype(BF)

    def outputs():
        @pl.loop(0, 8)
        def _(j):
            rows = dot(hid[...], w[2, j % 4, j // 4], 1, 1).astype(BF)
            px[:, :, :, shard(j)] = rows.reshape(NQ, NZ, S, SH)

    def act_grads():
        @pl.loop(0, 512 // RB)
        def _(i):
            rs = pl.ds(pl.multiple_of(i * RB, RB), RB)
            g, t = ga[rs, :], gh[rs, :]
            s = jax.nn.sigmoid(g)
            gu[rs, :] = (t * (g * s)).astype(BF)
            gg[rs, :] = (t * ua[rs, :] * s * (1.0 + g * (1.0 - s))).astype(BF)

    def row_grads():
        @pl.loop(0, 8)
        def _(j):
            rows = dot(gg[...], w[0, j % 4, j // 4], 1, 1) + dot(gu[...], w[1, j % 4, j // 4], 1, 1)
            pg[:, :, :, shard(j)] = rows.astype(BF).reshape(NQ, NZ, S, SH)

    def yback(a, src, dst, k):
        t = (q + k) % NQ
        return remote(src.at[t], dst.at[q], ys.at[2 + a, k], yr.at[2 + a, k], dev_q(t))

    def back_start(a):
        src, dst = (px, ro) if a == 0 else (pg, rr)
        for k in range(1, NQ):
            yback(a, src, dst, k).start()
        dst[q] = src[q]

    def back_wait(a):
        src, dst = (px, ro) if a == 0 else (pg, rr)
        for k in range(1, NQ):
            yback(a, src, dst, k).wait_recv()

    def slots_sent(a):
        src, dst = (px, xr) if a == 0 else (pg, gr)
        for k in range(1, NQ):
            ywhole(a, src, dst, k).wait_send()

    pairs = ((xr, gg), (xr, gu), (gr, hid))

    def zof(i):
        return zo if i == 0 else zhi

    def grads(m, xx, i):
        left, right = pairs[m]
        wgr[m, xx, zof(i)] = dot(rows_by(left, zof(i) * 4 + xx), right[...], 0, 0).astype(BF)

    A, B = pl.ds(0, HF), pl.ds(HF, HF)

    def gcopy(m, i, kind):
        sems = (qs.at[m, i, kind], qr.at[m, i, kind])
        zh = zof(i)
        if kind == 0:
            return remote(wgr.at[m, xo, zh, A], r2.at[m, 0, i], *sems, dev_xp)
        if kind == 1:
            return remote(wgr.at[m, xo, zh, B], r2.at[m, 1, i], *sems, dev_xm)
        if kind == 2:
            return remote(wgr.at[m, xp, zh, B], r1.at[m, 0, i, B], *sems, dev_xp)
        if kind == 3:
            return remote(wgr.at[m, xm, zh, A], r1.at[m, 1, i, A], *sems, dev_xm)
        if kind == 4:
            return remote(wgr.at[m, xp, zh, A], r1.at[m, 0, i, A], *sems, dev_xp)
        if kind == 5:
            return remote(wgr.at[m, xm, zh, B], r1.at[m, 1, i, B], *sems, dev_xm)
        return remote(wgr.at[m, x, zh], rz.at[m], *sems, dev_zo)

    def scatter(m, i):
        grads(m, xo, i)
        gcopy(m, i, 0).start()
        gcopy(m, i, 1).start()
        grads(m, xp, i)
        gcopy(m, i, 2).start()
        grads(m, xm, i)
        gcopy(m, i, 3).start()

    def merge(m, i):
        zh = zof(i)
        gcopy(m, i, 0).wait_recv()
        wgr[m, xp, zh, A] = (wgr[m, xp, zh, A].astype(F32) + r2[m, 0, i].astype(F32)).astype(BF)
        gcopy(m, i, 4).start()
        gcopy(m, i, 1).wait_recv()
        wgr[m, xm, zh, B] = (wgr[m, xm, zh, B].astype(F32) + r2[m, 1, i].astype(F32)).astype(BF)
        gcopy(m, i, 5).start()

    outs = (dg_ref, du_ref, dd_ref)
    turn = (2, 0, 1)

    def collect(m):
        for kind in (2, 3, 4, 5):
            gcopy(m, 0, kind).wait_recv()
        wgr[m, x, zo] = (
            wgr[m, x, zo].astype(F32) + r1[m, 0, 0].astype(F32) + r1[m, 1, 0].astype(F32)
        ).astype(BF)
        gcopy(m, 0, 6).start()

    def finish(m):
        for kind in (2, 3, 4, 5):
            gcopy(m, 1, kind).wait_recv()
        gcopy(m, 0, 6).wait_recv()
        outs[m][...] = (
            wgr[m, x, zhi].astype(F32) + r1[m, 0, 1].astype(F32)
            + r1[m, 1, 1].astype(F32) + rz[m].astype(F32)
        ).astype(BF)

    def spread(a, b):
        p0, p1 = places(b)
        src, dst = (ro, tb) if a == 0 else (rr, tp)
        if a == 0:
            pw = p0 * mb[b, 2:3, :] + p1 * mb[b, 3:4, :]
            high = pw.astype(BF)
            low = (pw - high.astype(F32)).astype(BF)

            def near(j, acc):
                cols = pl.ds(pl.multiple_of(j * CC, CC), CC)
                return acc + dot(src[:, b, :, cols].reshape(TOK, CC), ob[b, :, cols], 1, 1)

            inner = lax.fori_loop(0, D // CC, near, jnp.zeros((TOK, TOK), F32))
            rgb[b, 2:8, :] = jnp.zeros((6, TOK), F32)
            rgb[b, 0:1, :] = jnp.sum(p0 * inner, axis=0, keepdims=True)
            rgb[b, 1:2, :] = jnp.sum(p1 * inner, axis=0, keepdims=True)
        else:
            high = (p0 + p1).astype(BF)

        @pl.loop(0, D // CC)
        def _(j):
            cols = pl.ds(pl.multiple_of(j * CC, CC), CC)
            rows = src[:, b, :, cols].reshape(TOK, CC)
            total = dot(high, rows, 0, 0)
            if a == 0:
                total = total + dot(low, rows, 0, 0)
            dst[b, :, cols] = total.astype(BF)

    def vcopy(a, n):
        buf = tb if a == 0 else tp
        slot = {3: 0, 2: 1, 1: 2}[n]
        return remote(buf.at[n], rv.at[a, slot], vs.at[a, n], vr.at[a, slot], dev_z(1 if n == 2 else -1))

    def vout(a):
        spread(a, 3)
        vcopy(a, 3).start()
        spread(a, 2)
        vcopy(a, 2).start()
        spread(a, 1)
        spread(a, 0)

    def vmerge(a):
        buf = tb if a == 0 else tp
        vcopy(a, 3).wait_recv()
        buf[1] = (buf[1].astype(F32) + rv[a, 0].astype(F32)).astype(BF)
        vcopy(a, 1).start()

    def vend(a, out):
        buf = tb if a == 0 else tp
        vcopy(a, 2).wait_recv()
        vcopy(a, 1).wait_recv()
        out[...] = (buf[0].astype(F32) + rv[a, 1].astype(F32) + rv[a, 2].astype(F32)).astype(BF)

    def rgcopy(k):
        return remote(rgb.at[k], rgr.at[k], gs.at[k], grs.at[k], dev_z((-1, 1, -2)[k - 1]))

    def rgsend():
        for k in range(1, NZ):
            rgcopy(k).start()

    def rgend():
        for k in range(1, NZ):
            rgcopy(k).wait_recv()
        rg_ref[...] = rgb[0, 0:2, :] + rgr[1, 0:2, :] + rgr[2, 0:2, :] + rgr[3, 0:2, :]

    def meta_wait():
        for k in range(1, NZ):
            mcopy(k).wait_recv()

    def local_wait(k):
        local[k].wait()

    local_wait(0)
    pack(0, 0)
    meta_wait()
    line_step(0, 1)
    wcopy(1, 2).start()
    pack(0, 1)
    line_step(0, 2)
    pack(0, 2)
    wforward(0, 0)
    line_step(0, 3)
    wcopy(2, 2).start()
    pack(0, 3)
    wforward(1, 0)
    wpartner(0)
    line_start(1)
    local_wait(1)
    pack(1, 0)
    wforward(2, 0)
    wpartner(1)
    wforward(0, 1)
    line_step(1, 1)
    pack(1, 1)
    ywait(0, px, xr)
    local_wait(2)
    wlast(0)
    through(ga, xr, 0)
    wpartner(2)
    wforward(1, 1)
    line_step(1, 2)
    pack(1, 2)
    local_wait(3)
    wlast(1)
    through(ua, xr, 1)
    hidden_rows()
    line_step(1, 3)
    pack(1, 3)
    wforward(2, 1)
    slots_sent(0)
    local_wait(4)
    wlast(2)
    outputs()
    back_start(0)
    ywait(1, pg, gr)
    scatter(2, 0)
    scatter(2, 1)
    through(gh, gr, 2)
    act_grads()
    scatter(0, 0)
    scatter(1, 0)
    slots_sent(1)
    row_grads()
    back_start(1)
    merge(2, 0)
    merge(2, 1)
    scatter(0, 1)
    scatter(1, 1)
    line_end(0)
    back_wait(0)
    vout(0)
    rgsend()
    merge(0, 0)
    merge(1, 0)
    for m in turn:
        grads(m, x, 0)
    collect(2)
    vmerge(0)
    merge(0, 1)
    merge(1, 1)
    back_wait(1)
    vout(1)
    collect(0)
    vmerge(1)
    collect(1)
    for m in turn:
        grads(m, x, 1)
    vend(0, lo_ref)
    rgend()
    vend(1, tg_ref)
    for m in turn:
        finish(m)

    line_end(1)
    for k in range(1, NZ):
        mcopy(k).wait_send()
        rgcopy(k).wait_send()
    for k in range(1, NQ):
        yback(0, px, ro, k).wait_send()
        yback(1, pg, rr, k).wait_send()
    for n in range(1, NZ):
        vcopy(0, n).wait_send()
        vcopy(1, n).wait_send()
    for m in range(3):
        for kind in (0, 1, 2, 3, 4, 7, 8, 9, 10):
            wcopy(m, kind).wait_send()
        for kind in range(7):
            gcopy(m, 0, kind).wait_send()
            if kind < 6:
                gcopy(m, 1, kind).wait_send()


def step(tokens, gate_weights, expert_ids, hot_experts, gate_proj, up_proj, down_proj, out_grad):
    hbm = pl.BlockSpec(memory_space=pl.ANY)
    vmem = pl.BlockSpec(memory_space=pltpu.VMEM)
    smem = pl.BlockSpec(memory_space=pltpu.SMEM)
    rows4 = (NQ, NZ, S, D)
    dma = pltpu.SemaphoreType.DMA
    scratch = [
        pltpu.VMEM((NZ, TOK, D), BF),
        pltpu.VMEM((NZ, TOK, D), BF),
        pltpu.VMEM((NZ, 8, TOK), F32),
        pltpu.VMEM(rows4, BF),
        pltpu.VMEM(rows4, BF),
        pltpu.VMEM(rows4, BF),
        pltpu.VMEM(rows4, BF),
        pltpu.VMEM((3, 4, 2, SH, FF), BF),
        pltpu.VMEM((512, FF), F32),
        pltpu.VMEM((512, FF), F32),
        pltpu.VMEM((512, FF), F32),
        pltpu.VMEM((512, FF), BF),
        pltpu.VMEM((512, FF), BF),
        pltpu.VMEM((512, FF), BF),
        pltpu.VMEM(rows4, BF),
        pltpu.VMEM(rows4, BF),
        pltpu.VMEM((NZ, TOK, D), BF),
        pltpu.VMEM((2, 3, TOK, D), BF),
        pltpu.VMEM((NZ, 8, TOK), F32),
        pltpu.VMEM((NZ, 8, TOK), F32),
        pltpu.VMEM((3, 4, 2, SH, FF), BF),
        pltpu.VMEM((3, 2, 2, HF, FF), BF),
        pltpu.VMEM((3, 2, 2, SH, FF), BF),
        pltpu.VMEM((3, SH, FF), BF),
        dma((5,)),
        dma((2, NZ)),
        dma((2, NZ)),
        dma((NZ,)),
        dma((NZ,)),
        dma((4, NQ)),
        dma((4, NQ)),
        dma((2, NZ)),
        dma((2, NZ)),
        dma((NZ,)),
        dma((NZ,)),
        dma((3, 11)),
        dma((3, 11)),
        dma((3, 2, 7)),
        dma((3, 2, 7)),
    ]
    shard = jax.ShapeDtypeStruct((SH, FF), BF)
    lo, tg, rg, dg, du, dd = pl.pallas_call(
        kernel,
        out_shape=(
            jax.ShapeDtypeStruct((TOK, D), BF),
            jax.ShapeDtypeStruct((TOK, D), BF),
            jax.ShapeDtypeStruct((2, TOK), F32),
            shard,
            shard,
            shard,
        ),
        in_specs=[smem, vmem, vmem, hbm, hbm, hbm, hbm, hbm],
        out_specs=(vmem,) * 6,
        scratch_shapes=scratch,
        compiler_params=pltpu.CompilerParams(
            collective_id=0, has_side_effects=True, vmem_limit_bytes=64 << 20
        ),
    )(
        hot_experts, expert_ids.T, gate_weights.T, tokens, out_grad,
        gate_proj[0], up_proj[0], down_proj[0],
    )
    return lo, tg, rg.T, dg[None], du[None], dd[None]


def solution(mesh):
    rows = P(("dp", "expert"), None)
    mats = P("expert", "dp", None)
    return jax.shard_map(
        step,
        mesh=mesh,
        in_specs=(rows, rows, rows, P(), mats, mats, mats, rows),
        out_specs=(rows, rows, rows, mats, mats, mats),
        check_vma=False,
    )
```

time: 322 us -> 259 us (0.80)
  Pallas kernels: 315 us -> 249 us
    pallas_call x1, Pallas kernels: 315 us -> 249 us  [step(): pl.pallas_call(kernel, out_shape=(jax.ShapeDtypeStruct((TOK, D), BF), jax...]
where the time goes in v2:
time: 259 us; the launch traced here: 256 us
  Pallas kernels  249 us (96%)
  local copies, waits for them, and re-layouts  6.32 us (2%)
    pallas_call x1, Pallas kernels, step(): pl.pallas_call(kernel, out_shape=(jax.ShapeDtypeStruct((TOK, D), BF), jax...  249 us
    unnamed x16, local copies, waits for them, and re-layouts  6.32 us

profile of v2, /device:TPU:1, one launch (start us, length us, event | category | flops | bytes accessed | tf_op | source)
XLA Modules:
  0.0 255.8 jit_solution(3127045695702537795)
XLA Ops:
  0.6 248.8 %shard_map.127 = (bf16[128,2048]{1,0:T(8,128)(2,1)}, bf16[128,2048]{1,0:T(8,128)(2,1)}, f32[2,128]{1,0:T(2,128)}, bf16[256,768]{1,0:T(8,128)(2,1)}, bf16[256,768]{1,0:T(8,128)(2,1)}, /*index=5*/bf16[256,768]{1,0:T(8,128)(2,1)}) custom-call(s32[4]{0:T(128)} %hot_ref.1, s32[2,128]{1,0:T(2,128)} %bitcast.15, f32[2,128]{1,0:T(2,128)} %bitcast.16, ...), custom_call_target="tpu_custom_call" | custom-call | tf_op jit(solution)/shard_map/pallas_call | solution.py:551
  249.5 0.0 copy-start
  249.5 1.9 copy.20
  251.4 0.0 copy-done
  251.4 0.0 copy-start.4
  251.4 0.0 copy-start.3
  251.4 0.8 copy.21
  252.2 0.0 copy-done.4
  252.2 0.6 copy.22
  252.8 0.0 copy-done.3
  252.8 0.0 copy-start.2
  252.8 0.7 copy.23
  253.5 0.4 copy-done.2
  253.9 0.0 copy-start.1
  253.9 0.7 copy.24
  254.7 0.4 copy-done.1
  255.0 0.7 copy.25
Async XLA Ops:
  249.5 2.0 copy-start
  251.4 0.8 copy-start.4
  251.4 1.4 copy-start.3
  252.8 1.1 copy-start.2
  253.9 1.1 copy-start.1

commit v3 on v2

--- a/solution.py
+++ b/solution.py
@@ -332,9 +332,6 @@
         p0, p1 = places(b)
         src, dst = (ro, tb) if a == 0 else (rr, tp)
         if a == 0:
-            pw = p0 * mb[b, 2:3, :] + p1 * mb[b, 3:4, :]
-            high = pw.astype(BF)
-            low = (pw - high.astype(F32)).astype(BF)
 
             def near(j, acc):
                 cols = pl.ds(pl.multiple_of(j * CC, CC), CC)
@@ -344,17 +341,19 @@
             rgb[b, 2:8, :] = jnp.zeros((6, TOK), F32)
             rgb[b, 0:1, :] = jnp.sum(p0 * inner, axis=0, keepdims=True)
             rgb[b, 1:2, :] = jnp.sum(p1 * inner, axis=0, keepdims=True)
+            pw = jnp.transpose(p0 * mb[b, 2:3, :] + p1 * mb[b, 3:4, :])
+            high = pw.astype(BF)
+            mix = jnp.concatenate([high, (pw - high.astype(F32)).astype(BF)], axis=1)
         else:
-            high = (p0 + p1).astype(BF)
+            mix = jnp.transpose(p0 + p1).astype(BF)
 
         @pl.loop(0, D // CC)
         def _(j):
             cols = pl.ds(pl.multiple_of(j * CC, CC), CC)
             rows = src[:, b, :, cols].reshape(TOK, CC)
-            total = dot(high, rows, 0, 0)
             if a == 0:
-                total = total + dot(low, rows, 0, 0)
-            dst[b, :, cols] = total.astype(BF)
+                rows = jnp.concatenate([rows, rows], axis=0)
+            dst[b, :, cols] = dot(mix, rows).astype(BF)
 
     def vcopy(a, n):
         buf = tb if a == 0 else tp
@@ -404,82 +403,84 @@
     pack(0, 0)
     meta_wait()
     line_step(0, 1)
-    wcopy(1, 2).start()
     pack(0, 1)
     line_step(0, 2)
+    wcopy(1, 2).start()
     pack(0, 2)
     wforward(0, 0)
     line_step(0, 3)
-    wcopy(2, 2).start()
     pack(0, 3)
-    wforward(1, 0)
     wpartner(0)
     line_start(1)
+    wforward(1, 0)
+    wforward(2, 0)
     local_wait(1)
     pack(1, 0)
-    wforward(2, 0)
     wpartner(1)
+    wcopy(2, 2).start()
     wforward(0, 1)
-    line_step(1, 1)
-    pack(1, 1)
     ywait(0, px, xr)
     local_wait(2)
     wlast(0)
     through(ga, xr, 0)
+    wforward(1, 1)
+    line_step(1, 1)
+    pack(1, 1)
     wpartner(2)
-    wforward(1, 1)
-    line_step(1, 2)
-    pack(1, 2)
     local_wait(3)
     wlast(1)
     through(ua, xr, 1)
     hidden_rows()
+    line_step(1, 2)
+    pack(1, 2)
     line_step(1, 3)
     pack(1, 3)
     wforward(2, 1)
+    ywait(1, pg, gr)
+    scatter(2, 0)
     slots_sent(0)
     local_wait(4)
     wlast(2)
     outputs()
     back_start(0)
-    ywait(1, pg, gr)
-    scatter(2, 0)
-    scatter(2, 1)
     through(gh, gr, 2)
     act_grads()
     scatter(0, 0)
+    merge(2, 0)
     scatter(1, 0)
     slots_sent(1)
     row_grads()
     back_start(1)
-    merge(2, 0)
-    merge(2, 1)
-    scatter(0, 1)
-    scatter(1, 1)
+    grads(2, x, 0)
+    merge(0, 0)
+    merge(1, 0)
+    collect(2)
+    scatter(2, 1)
     line_end(0)
     back_wait(0)
     vout(0)
     rgsend()
-    merge(0, 0)
-    merge(1, 0)
-    for m in turn:
-        grads(m, x, 0)
-    collect(2)
-    vmerge(0)
+    scatter(0, 1)
+    merge(2, 1)
+    grads(0, x, 0)
+    collect(0)
+    scatter(1, 1)
+    grads(1, x, 0)
+    collect(1)
     merge(0, 1)
     merge(1, 1)
+    vmerge(0)
     back_wait(1)
     vout(1)
-    collect(0)
-    vmerge(1)
-    collect(1)
     for m in turn:
         grads(m, x, 1)
+    vmerge(1)
     vend(0, lo_ref)
     rgend()
+    finish(2)
     vend(1, tg_ref)
-    for m in turn:
-        finish(m)
+    finish(0)
+    finish(1)
 
     line_end(1)
     for k in range(1, NZ):

time: 259 us -> 242 us (0.934); the launches traced: 256 us -> 242 us
  Pallas kernels: 249 us -> 235 us
    pallas_call x1, Pallas kernels: 249 us -> 235 us  [step(): pl.pallas_call(kernel, out_shape=(jax.ShapeDtypeStruct((TOK, D), BF), jax...]
where the time goes in v3:
time: 242 us
  Pallas kernels  235 us (97%)
  local copies, waits for them, and re-layouts  6.32 us (3%)
    pallas_call x1, Pallas kernels, step(): pl.pallas_call(kernel, out_shape=(jax.ShapeDtypeStruct((TOK, D), BF), jax...  235 us
    unnamed x16, local copies, waits for them, and re-layouts  6.32 us

profile of v3, /device:TPU:1, one launch (start us, length us, event | category | flops | bytes accessed | tf_op | source)
XLA Modules:
  0.0 241.6 jit_solution(14057987472449495566)
XLA Ops:
  0.6 234.6 %shard_map.127 = (bf16[128,2048]{1,0:T(8,128)(2,1)}, bf16[128,2048]{1,0:T(8,128)(2,1)}, f32[2,128]{1,0:T(2,128)}, bf16[256,768]{1,0:T(8,128)(2,1)}, bf16[256,768]{1,0:T(8,128)(2,1)}, /*index=5*/bf16[256,768]{1,0:T(8,128)(2,1)}) custom-call(s32[4]{0:T(128)} %hot_ref.1, s32[2,128]{1,0:T(2,128)} %bitcast.15, f32[2,128]{1,0:T(2,128)} %bitcast.16, ...), custom_call_target="tpu_custom_call" | custom-call | tf_op jit(solution)/shard_map/pallas_call | solution.py:552
  235.2 0.0 copy-start
  235.3 1.9 copy.20
  237.2 0.0 copy-done
  237.2 0.0 copy-start.4
  237.2 0.0 copy-start.3
  237.2 0.8 copy.21
  238.0 0.0 copy-done.4
  238.0 0.6 copy.22
  238.6 0.0 copy-done.3
  238.6 0.0 copy-start.2
  238.6 0.7 copy.23
  239.3 0.4 copy-done.2
  239.7 0.0 copy-start.1
  239.7 0.7 copy.24
  240.5 0.4 copy-done.1
  240.8 0.7 copy.25
Async XLA Ops:
  235.2 2.0 copy-start
  237.2 0.8 copy-start.4
  237.2 1.4 copy-start.3
  238.6 1.1 copy-start.2
  239.7 1.1 copy-start.1

commit v4 on v3

--- a/solution.py
+++ b/solution.py
@@ -441,20 +441,20 @@
     slots_sent(0)
     local_wait(4)
     wlast(2)
-    outputs()
-    back_start(0)
     through(gh, gr, 2)
     act_grads()
     scatter(0, 0)
     merge(2, 0)
     scatter(1, 0)
+    outputs()
+    back_start(0)
+    grads(2, x, 0)
+    collect(2)
     slots_sent(1)
     row_grads()
     back_start(1)
-    grads(2, x, 0)
     merge(0, 0)
     merge(1, 0)
-    collect(2)
     scatter(2, 1)
     line_end(0)
     back_wait(0)

time: 242 us -> 239 us (0.988)
  Pallas kernels: 235 us -> 232 us
    pallas_call x1, Pallas kernels: 235 us -> 232 us  [step(): pl.pallas_call(kernel, out_shape=(jax.ShapeDtypeStruct((TOK, D), BF), jax...]
where the time goes in v4:
time: 239 us
  Pallas kernels  232 us (97%)
  local copies, waits for them, and re-layouts  6.32 us (3%)
    pallas_call x1, Pallas kernels, step(): pl.pallas_call(kernel, out_shape=(jax.ShapeDtypeStruct((TOK, D), BF), jax...  232 us
    unnamed x16, local copies, waits for them, and re-layouts  6.32 us

profile of v4, /device:TPU:1, one launch (start us, length us, event | category | flops | bytes accessed | tf_op | source)
XLA Modules:
  0.0 239.1 jit_solution(15533268328288005323)
XLA Ops:
  0.6 232.1 %shard_map.127 = (bf16[128,2048]{1,0:T(8,128)(2,1)}, bf16[128,2048]{1,0:T(8,128)(2,1)}, f32[2,128]{1,0:T(2,128)}, bf16[256,768]{1,0:T(8,128)(2,1)}, bf16[256,768]{1,0:T(8,128)(2,1)}, /*index=5*/bf16[256,768]{1,0:T(8,128)(2,1)}) custom-call(s32[4]{0:T(128)} %hot_ref.1, s32[2,128]{1,0:T(2,128)} %bitcast.15, f32[2,128]{1,0:T(2,128)} %bitcast.16, ...), custom_call_target="tpu_custom_call" | custom-call | tf_op jit(solution)/shard_map/pallas_call | solution.py:552
  232.8 0.0 copy-start
  232.8 1.9 copy.20
  234.7 0.0 copy-done
  234.7 0.0 copy-start.4
  234.7 0.0 copy-start.3
  234.7 0.8 copy.21
  235.5 0.0 copy-done.4
  235.5 0.6 copy.22
  236.1 0.0 copy-done.3
  236.1 0.0 copy-start.2
  236.1 0.7 copy.23
  236.9 0.4 copy-done.2
  237.2 0.0 copy-start.1
  237.2 0.7 copy.24
  238.0 0.4 copy-done.1
  238.4 0.7 copy.25
Async XLA Ops:
  232.8 2.0 copy-start
  234.7 0.8 copy-start.4
  234.7 1.4 copy-start.3
  236.1 1.1 copy-start.2
  237.2 1.1 copy-start.1
